TPU v7x, 32 devices: a whole 2x2x4 slice. The times are simulated.
32 devices in a mesh: row: 4 (over y, core), col: 8 (over z, x).
Axes of the slice: x: 2, y: 2, z: 4, core: 2. Of those that a mesh axis runs over, the one named last changes fastest.
Arguments:
- factor: bfloat16 [4, 10, 512, 8, 512], P('row', None, None, 'col'), may hold values from -0.09375 to 0.09375
- dinv: bfloat16 [4, 2, 512, 512], P('row'), may hold values from -1 to 2, as said below
- rhs: float32 [4, 10, 64, 512], P('row'), may hold values from -6 to 6
Outputs:
- result: float32 [4, 10, 64, 512], P('row')
Inputs may be any that keep to these rules, and one draw needn't show every extreme that they name: dinv holds the given inverses of the window's diagonal tiles; they are dense and stored apart, and factor's tiles at and below the diagonal (block row i >= 32 + j in window column j) are never read.
All inputs are finite; a program needn't handle non-finite values.
Results may differ from a plain program's by a relative error of at most 0.0028.
Values may be sent and summed in bfloat16 or wider, within the bound.
A program may use at most 64 MiB of HBM per device.

v0:
```python
import jax
import jax.numpy as jnp
from jax import lax
from jax.sharding import PartitionSpec as P


def from_root(array, axis, root):
    mine = lax.axis_index(axis) == root
    return lax.psum(jnp.where(mine, array, jnp.zeros_like(array)), axis)


def shards(factor, dinv, rhs):
    grid_rows = lax.axis_size("row")
    grid_cols = lax.axis_size("col")
    row_index = lax.axis_index("row")
    col_index = lax.axis_index("col")
    factor_tiles = factor[0, :, :, 0, :]
    inverse = dinv[0]
    local_rhs = rhs[0]
    held_rows = factor_tiles.shape[0]
    held_diag = inverse.shape[0]
    lead_rows = held_rows - held_diag
    offset = lead_rows * grid_rows
    block_ids = jnp.arange(held_rows, dtype=jnp.int32) * grid_rows + row_index

    def one_step(counter, carried):
        partials, results = carried
        column = grid_cols - 1 - counter
        target = offset + column
        tile_slot = target // grid_rows
        owner_row = column % grid_rows
        summed = lax.psum(partials[tile_slot], "col")
        y_block = local_rhs[tile_slot] - summed
        tile_inv = inverse[column // grid_rows]
        x_block = jnp.dot(
            y_block,
            tile_inv.astype(jnp.float32).T,
            precision=lax.Precision.HIGHEST,
            preferred_element_type=jnp.float32,
        )
        x_round = from_root(x_block.astype(jnp.bfloat16), "row", owner_row)
        results = results.at[tile_slot].set(
            jnp.where(row_index == owner_row, x_block, results[tile_slot])
        )

        def accumulate(running):
            products = jnp.einsum(
                "nb,iab->ina", x_round, factor_tiles, preferred_element_type=jnp.float32
            )
            return running + jnp.where(
                (block_ids < target)[:, None, None], products, jnp.float32(0.0)
            )

        def unchanged(running):
            return running

        partials = lax.cond(col_index == column, accumulate, unchanged, partials)
        return (partials, results)

    start_sums = jnp.zeros(local_rhs.shape, jnp.float32)
    partials, results = lax.fori_loop(0, grid_cols, one_step, (start_sums, local_rhs))
    leading = lax.psum(partials[:lead_rows], "col")
    results = results.at[:lead_rows].set(local_rhs[:lead_rows] - leading)
    return results[None]


def solution(mesh):
    in_specs = (
        P("row", None, None, "col", None),
        P("row", None, None, None),
        P("row", None, None, None),
    )
    out_specs = P("row", None, None, None)
    return jax.shard_map(shards, mesh=mesh, in_specs=in_specs, out_specs=out_specs, check_vma=False)
```

profile of v0, /device:TPU:8, one launch (start us, length us, event | category | flops | bytes accessed | tf_op | source)
XLA Modules:
  0.0 979.2 jit_solution(6265109136219580719)
XLA Ops:
  7.4 2.5 copy.11
  10.0 1.2 copy-done
  11.2 876.6 %while.25 = (s32[]{:T(128)}, f32[10,64,512]{2,1,0:T(8,128)S(1)}, f32[10,64,512]{2,1,0:T(8,128)}, s32[]{:T(128)}, f32[10,64,512]{2,1,0:T(8,128)S(1)}, /*index=5*/...) while((s32[]{:T(128)}, f32[10,64,512]{2,1,0:T(8,128)S(1)}, ...), condition=%wide.region_6.7_spmd.clone.clone, body=%wide.region_0.6_spmd.clone.clone.sunk | while | flops 537755712 | bytes 11012557 | solution.py:61
  12.6 0.9 constant_dynamic-slice_fusion.2
  13.6 72.6 %all-reduce.6.cloned.1.call-done = f32[64,512]{1,0:T(8,128)} async-done(((f32[64,512]{1,0:T(8,128)}), f32[64,512]{1,0:T(8,128)}) %all-reduce.6.cloned.1.call-update) | async-done | bytes 131088 | tf_op jit(solution)/shard_map/while/body/eval_jaxpr/psum | solution.py:32
  86.1 2.3 convert_select_fusion.2
  88.5 1.3 fusion.14
  89.8 29.7 %all-reduce.8.cloned.1.call-done = bf16[64,512]{1,0:T(8,128)(2,1)} async-done(((bf16[64,512]{1,0:T(8,128)(2,1)}), bf16[64,512]{1,0:T(8,128)(2,1)}) %all-reduce.8.cloned.1.call-update) | async-done | bytes 65552 | tf_op jit(solution)/shard_map/while/body/eval_jaxpr/psum | solution.py:9
  121.0 0.9 constant_dynamic-slice_fusion.2
  121.9 75.6 %all-reduce.6.cloned.1.call-done = f32[64,512]{1,0:T(8,128)} async-done(((f32[64,512]{1,0:T(8,128)}), f32[64,512]{1,0:T(8,128)}) %all-reduce.6.cloned.1.call-update) | async-done | bytes 131088 | tf_op jit(solution)/shard_map/while/body/eval_jaxpr/psum | solution.py:32
  197.5 2.3 convert_select_fusion.2
  199.9 1.3 fusion.14
  201.2 29.7 %all-reduce.8.cloned.1.call-done = bf16[64,512]{1,0:T(8,128)(2,1)} async-done(((bf16[64,512]{1,0:T(8,128)(2,1)}), bf16[64,512]{1,0:T(8,128)(2,1)}) %all-reduce.8.cloned.1.call-update) | async-done | bytes 65552 | tf_op jit(solution)/shard_map/while/body/eval_jaxpr/psum | solution.py:9
  232.3 0.9 constant_dynamic-slice_fusion.2
  233.3 74.5 %all-reduce.6.cloned.1.call-done = f32[64,512]{1,0:T(8,128)} async-done(((f32[64,512]{1,0:T(8,128)}), f32[64,512]{1,0:T(8,128)}) %all-reduce.6.cloned.1.call-update) | async-done | bytes 131088 | tf_op jit(solution)/shard_map/while/body/eval_jaxpr/psum | solution.py:32
  307.7 2.3 convert_select_fusion.2
  310.1 1.3 fusion.14
  311.4 29.7 %all-reduce.8.cloned.1.call-done = bf16[64,512]{1,0:T(8,128)(2,1)} async-done(((bf16[64,512]{1,0:T(8,128)(2,1)}), bf16[64,512]{1,0:T(8,128)(2,1)}) %all-reduce.8.cloned.1.call-update) | async-done | bytes 65552 | tf_op jit(solution)/shard_map/while/body/eval_jaxpr/psum | solution.py:9
  342.6 0.9 constant_dynamic-slice_fusion.2
  343.5 74.7 %all-reduce.6.cloned.1.call-done = f32[64,512]{1,0:T(8,128)} async-done(((f32[64,512]{1,0:T(8,128)}), f32[64,512]{1,0:T(8,128)}) %all-reduce.6.cloned.1.call-update) | async-done | bytes 131088 | tf_op jit(solution)/shard_map/while/body/eval_jaxpr/psum | solution.py:32
  418.2 2.3 convert_select_fusion.2
  420.6 1.3 fusion.14
  421.9 29.7 %all-reduce.8.cloned.1.call-done = bf16[64,512]{1,0:T(8,128)(2,1)} async-done(((bf16[64,512]{1,0:T(8,128)(2,1)}), bf16[64,512]{1,0:T(8,128)(2,1)}) %all-reduce.8.cloned.1.call-update) | async-done | bytes 65552 | tf_op jit(solution)/shard_map/while/body/eval_jaxpr/psum | solution.py:9
  453.1 0.9 constant_dynamic-slice_fusion.2
  454.0 73.8 %all-reduce.6.cloned.1.call-done = f32[64,512]{1,0:T(8,128)} async-done(((f32[64,512]{1,0:T(8,128)}), f32[64,512]{1,0:T(8,128)}) %all-reduce.6.cloned.1.call-update) | async-done | bytes 131088 | tf_op jit(solution)/shard_map/while/body/eval_jaxpr/psum | solution.py:32
  527.8 2.3 convert_select_fusion.2
  530.2 1.3 fusion.14
  531.5 29.7 %all-reduce.8.cloned.1.call-done = bf16[64,512]{1,0:T(8,128)(2,1)} async-done(((bf16[64,512]{1,0:T(8,128)(2,1)}), bf16[64,512]{1,0:T(8,128)(2,1)}) %all-reduce.8.cloned.1.call-update) | async-done | bytes 65552 | tf_op jit(solution)/shard_map/while/body/eval_jaxpr/psum | solution.py:9
  562.7 0.9 constant_dynamic-slice_fusion.2
  563.6 73.8 %all-reduce.6.cloned.1.call-done = f32[64,512]{1,0:T(8,128)} async-done(((f32[64,512]{1,0:T(8,128)}), f32[64,512]{1,0:T(8,128)}) %all-reduce.6.cloned.1.call-update) | async-done | bytes 131088 | tf_op jit(solution)/shard_map/while/body/eval_jaxpr/psum | solution.py:32
  637.4 2.3 convert_select_fusion.2
  639.7 1.3 fusion.14
  641.0 29.7 %all-reduce.8.cloned.1.call-done = bf16[64,512]{1,0:T(8,128)(2,1)} async-done(((bf16[64,512]{1,0:T(8,128)(2,1)}), bf16[64,512]{1,0:T(8,128)(2,1)}) %all-reduce.8.cloned.1.call-update) | async-done | bytes 65552 | tf_op jit(solution)/shard_map/while/body/eval_jaxpr/psum | solution.py:9
  670.8 4.2 conditional.4
  670.8 4.2 fusion.3
  676.5 0.9 constant_dynamic-slice_fusion.2
  677.5 68.6 %all-reduce.6.cloned.1.call-done = f32[64,512]{1,0:T(8,128)} async-done(((f32[64,512]{1,0:T(8,128)}), f32[64,512]{1,0:T(8,128)}) %all-reduce.6.cloned.1.call-update) | async-done | bytes 131088 | tf_op jit(solution)/shard_map/while/body/eval_jaxpr/psum | solution.py:32
  746.1 2.3 convert_select_fusion.2
  748.4 1.3 fusion.14
  749.7 29.7 %all-reduce.8.cloned.1.call-done = bf16[64,512]{1,0:T(8,128)(2,1)} async-done(((bf16[64,512]{1,0:T(8,128)(2,1)}), bf16[64,512]{1,0:T(8,128)(2,1)}) %all-reduce.8.cloned.1.call-update) | async-done | bytes 65552 | tf_op jit(solution)/shard_map/while/body/eval_jaxpr/psum | solution.py:9
  780.9 0.9 constant_dynamic-slice_fusion.2
  781.8 72.6 %all-reduce.6.cloned.1.call-done = f32[64,512]{1,0:T(8,128)} async-done(((f32[64,512]{1,0:T(8,128)}), f32[64,512]{1,0:T(8,128)}) %all-reduce.6.cloned.1.call-update) | async-done | bytes 131088 | tf_op jit(solution)/shard_map/while/body/eval_jaxpr/psum | solution.py:32
  854.4 2.3 convert_select_fusion.2
  856.8 1.3 fusion.14
  858.1 29.7 %all-reduce.8.cloned.1.call-done = bf16[64,512]{1,0:T(8,128)(2,1)} async-done(((bf16[64,512]{1,0:T(8,128)(2,1)}), bf16[64,512]{1,0:T(8,128)(2,1)}) %all-reduce.8.cloned.1.call-update) | async-done | bytes 65552 | tf_op jit(solution)/shard_map/while/body/eval_jaxpr/psum | solution.py:9
  887.8 1.1 slice.68
  888.9 80.8 %all-reduce.4.cloned.1.call-done = f32[8,64,512]{2,1,0:T(8,128)} async-done(((f32[8,64,512]{2,1,0:T(8,128)}), f32[8,64,512]{2,1,0:T(8,128)}) %all-reduce.4.cloned.1.call-update) | async-done | bytes 1048592 | tf_op jit(solution)/shard_map/psum | solution.py:62
  969.6 2.4 bitcast_dynamic-update-slice_fusion
  (70 shorter events, 12.1 us)
Async XLA Ops:
  9.8 1.3 copy-start
  9.8 1.3 copy-start.1
  11.2 75.0 %all-reduce.6.cloned.1.call-start = ((), (), s32[]{:S(2)}) async-start(), calls=%async_computation.1 | async-start | bytes 262144 | tf_op jit(solution)/shard_map/while/body/eval_jaxpr/psum | solution.py:32
  11.9 107.6 %all-reduce.8.cloned.1.call-start = ((), (), s32[]{:S(2)}) async-start(), calls=%async_computation.2 | async-start | bytes 131072 | tf_op jit(solution)/shard_map/while/body/eval_jaxpr/psum | solution.py:9
  119.5 78.0 %all-reduce.6.cloned.1.call-start = ((), (), s32[]{:S(2)}) async-start(), calls=%async_computation.1 | async-start | bytes 262144 | tf_op jit(solution)/shard_map/while/body/eval_jaxpr/psum | solution.py:32
  120.2 110.7 %all-reduce.8.cloned.1.call-start = ((), (), s32[]{:S(2)}) async-start(), calls=%async_computation.2 | async-start | bytes 131072 | tf_op jit(solution)/shard_map/while/body/eval_jaxpr/psum | solution.py:9
  230.9 76.8 %all-reduce.6.cloned.1.call-start = ((), (), s32[]{:S(2)}) async-start(), calls=%async_computation.1 | async-start | bytes 262144 | tf_op jit(solution)/shard_map/while/body/eval_jaxpr/psum | solution.py:32
  231.6 109.5 %all-reduce.8.cloned.1.call-start = ((), (), s32[]{:S(2)}) async-start(), calls=%async_computation.2 | async-start | bytes 131072 | tf_op jit(solution)/shard_map/while/body/eval_jaxpr/psum | solution.py:9
  341.1 77.1 %all-reduce.6.cloned.1.call-start = ((), (), s32[]{:S(2)}) async-start(), calls=%async_computation.1 | async-start | bytes 262144 | tf_op jit(solution)/shard_map/while/body/eval_jaxpr/psum | solution.py:32
  341.8 109.8 %all-reduce.8.cloned.1.call-start = ((), (), s32[]{:S(2)}) async-start(), calls=%async_computation.2 | async-start | bytes 131072 | tf_op jit(solution)/shard_map/while/body/eval_jaxpr/psum | solution.py:9
  451.6 76.2 %all-reduce.6.cloned.1.call-start = ((), (), s32[]{:S(2)}) async-start(), calls=%async_computation.1 | async-start | bytes 262144 | tf_op jit(solution)/shard_map/while/body/eval_jaxpr/psum | solution.py:32
  452.3 108.9 %all-reduce.8.cloned.1.call-start = ((), (), s32[]{:S(2)}) async-start(), calls=%async_computation.2 | async-start | bytes 131072 | tf_op jit(solution)/shard_map/while/body/eval_jaxpr/psum | solution.py:9
  561.2 76.2 %all-reduce.6.cloned.1.call-start = ((), (), s32[]{:S(2)}) async-start(), calls=%async_computation.1 | async-start | bytes 262144 | tf_op jit(solution)/shard_map/while/body/eval_jaxpr/psum | solution.py:32
  561.9 108.8 %all-reduce.8.cloned.1.call-start = ((), (), s32[]{:S(2)}) async-start(), calls=%async_computation.2 | async-start | bytes 131072 | tf_op jit(solution)/shard_map/while/body/eval_jaxpr/psum | solution.py:9
  675.0 71.0 %all-reduce.6.cloned.1.call-start = ((), (), s32[]{:S(2)}) async-start(), calls=%async_computation.1 | async-start | bytes 262144 | tf_op jit(solution)/shard_map/while/body/eval_jaxpr/psum | solution.py:32
  675.8 103.7 %all-reduce.8.cloned.1.call-start = ((), (), s32[]{:S(2)}) async-start(), calls=%async_computation.2 | async-start | bytes 131072 | tf_op jit(solution)/shard_map/while/body/eval_jaxpr/psum | solution.py:9
  779.4 75.0 %all-reduce.6.cloned.1.call-start = ((), (), s32[]{:S(2)}) async-start(), calls=%async_computation.1 | async-start | bytes 262144 | tf_op jit(solution)/shard_map/while/body/eval_jaxpr/psum | solution.py:32
  780.1 107.7 %all-reduce.8.cloned.1.call-start = ((), (), s32[]{:S(2)}) async-start(), calls=%async_computation.2 | async-start | bytes 131072 | tf_op jit(solution)/shard_map/while/body/eval_jaxpr/psum | solution.py:9
  887.8 81.9 %all-reduce.4.cloned.1.call-start = ((), (), s32[]{:S(2)}) async-start(), calls=%async_computation | async-start | bytes 2097152 | tf_op jit(solution)/shard_map/psum | solution.py:62
Sparse Core Ops, SparseCore 0:
  15.7 70.3 all-reduce.5
  88.6 30.8 all-reduce.7
  124.0 73.4 all-reduce.5
  200.0 30.8 all-reduce.7
  235.1 72.5 all-reduce.5
  310.2 30.8 all-reduce.7
  345.7 72.5 all-reduce.5
  420.7 30.8 all-reduce.7
  456.1 71.6 all-reduce.5
  530.3 30.8 all-reduce.7
  565.7 71.5 all-reduce.5
  639.9 30.8 all-reduce.7
  679.6 66.4 all-reduce.5
  748.5 30.8 all-reduce.7
  783.7 70.6 all-reduce.5
  856.9 30.8 all-reduce.7
Sparse Core Ops, SparseCore 1:
  891.7 77.9 all-reduce.3
where the time goes:
time: 981 us; the launch traced here: 979 us
  waiting for transfers between devices  905 us (92%)
  matrix products  22.9 us (2%)
  other arithmetic  18.6 us (2%)
  local copies, waits for them, and re-layouts  17.3 us (2%)
  between operations  14.5 us (1%)
    psum x8, waiting for transfers between devices, one_step(): summed = lax.psum(partials[tile_slot], 'col')  586 us
    psum x8, waiting for transfers between devices, from_root(): return lax.psum(jnp.where(mine, array, jnp.zeros_like(array)), axis)  238 us
    psum x1, waiting for transfers between devices, shards(): leading = lax.psum(partials[:lead_rows], 'col')  80.8 us
  transfers between devices with their start and end apart: 17, of which 17 were waited for; matrix products, arithmetic and copies ran while one was open for 2% of the time, Pallas kernels for 0%

commit v1 on v0

v1 whole, which is shorter than its diff:
```python
import functools

import jax
import jax.numpy as jnp
from jax import lax
from jax.experimental import pallas as pl
from jax.experimental.pallas import tpu as pltpu
from jax.sharding import PartitionSpec as P

MESH = pl.DeviceIdType.MESH
F32 = jnp.float32
BF16 = jnp.bfloat16


def dot_nt(a, b):
    return lax.dot_general(a, b, (((1,), (1,)), ((), ())), preferred_element_type=F32)


def times_inverse(y, inv):
    n = y.shape[0]
    high = y.astype(BF16)
    low = (y - high.astype(F32)).astype(BF16)
    both = dot_nt(jnp.concatenate([high, low], axis=0), inv)
    return both[:n] + both[n:]


def kernel(
    grid_rows, grid_cols, lead, diag, nrhs, pieces,
    factor_in, inv_in, rhs_in, out,
    factor, inv, rhs, held, parts, part_out, lead_out, lead_in, sums, solved, y_acc,
    load_sem, x_send, x_recv, p_send, p_recv, l_send, l_recv, s_send, s_recv, r_send, r_recv,
):
    r = lax.axis_index("row")
    c = lax.axis_index("col")
    last = grid_cols - 1
    last_row, last_slot = last % grid_rows, last // grid_rows
    loads = [
        pltpu.make_async_copy(inv_in, inv, load_sem.at[0]),
        pltpu.make_async_copy(rhs_in, rhs, load_sem.at[1]),
        pltpu.make_async_copy(
            factor_in.at[pl.ds(lead, diag)], factor.at[pl.ds(lead, diag)], load_sem.at[2]
        ),
        pltpu.make_async_copy(
            factor_in.at[pl.ds(0, lead)], factor.at[pl.ds(0, lead)], load_sem.at[3]
        ),
    ]
    for load in loads:
        load.start()

    barrier = pltpu.get_barrier_semaphore()
    for step in range(1, grid_cols):
        pl.semaphore_signal(
            barrier, inc=1, device_id=(r, lax.rem(c + step, grid_cols)), device_id_type=MESH
        )
    for dr in range(1, grid_rows):
        for dc in (grid_cols - 1, 0, 1):
            pl.semaphore_signal(
                barrier,
                inc=1,
                device_id=(lax.rem(r + dr, grid_rows), lax.rem(c + dc, grid_cols)),
                device_id_type=MESH,
            )
    pl.semaphore_wait(barrier, grid_cols - 1 + 3 * (grid_rows - 1))

    def x_copy(src, row, col):
        return pltpu.make_async_remote_copy(
            src_ref=src, dst_ref=held, send_sem=x_send.at[row], recv_sem=x_recv,
            device_id=(row, col), device_id_type=MESH,
        )

    def part_copy(d, src_col, dst_col):
        return pltpu.make_async_remote_copy(
            src_ref=part_out.at[d], dst_ref=parts.at[src_col], send_sem=p_send.at[d],
            recv_sem=p_recv.at[src_col], device_id=(r, dst_col), device_id_type=MESH,
        )

    def lead_copy(piece, src_col):
        return pltpu.make_async_remote_copy(
            src_ref=lead_out.at[piece], dst_ref=lead_in.at[src_col], send_sem=l_send.at[piece],
            recv_sem=l_recv.at[src_col], device_id=(r, piece), device_id_type=MESH,
        )

    def sum_copy(src_col, dst_col):
        return pltpu.make_async_remote_copy(
            src_ref=sums.at[src_col], dst_ref=sums.at[src_col], send_sem=s_send.at[dst_col],
            recv_sem=s_recv.at[src_col], device_id=(r, dst_col), device_id_type=MESH,
        )

    def solved_copy(d, dst_col):
        return pltpu.make_async_remote_copy(
            src_ref=solved.at[d], dst_ref=solved.at[d], send_sem=r_send.at[dst_col],
            recv_sem=r_recv.at[d], device_id=(r, dst_col), device_id_type=MESH,
        )

    first_owner = jnp.logical_and(r == last_row, c == last)
    loads[0].wait()
    loads[1].wait()

    @pl.when(r == last_row)
    def _():
        solved[last_slot] = times_inverse(rhs[lead + last_slot], inv[last_slot]).astype(BF16)

    @pl.when(first_owner)
    def _():
        for dr in range(1, grid_rows):
            x_copy(solved.at[last_slot], (last_row + dr) % grid_rows, last).start()
        held[...] = solved[last_slot]

    loads[2].wait()

    k = c - 1
    solver = jnp.logical_and(c >= 1, r == lax.rem(k + grid_rows, grid_rows))
    kd = lax.div(jnp.maximum(k, 0), grid_rows)

    @pl.when(solver)
    def _():
        y_acc[...] = rhs[lead + kd]

        def add(step, carry):
            src = last - step
            part_copy(0, src, c).wait_recv()
            y_acc[...] -= parts[src].astype(F32)
            return carry

        lax.fori_loop(0, jnp.maximum(last - c - 1, 0), add, 0)

    @pl.when(jnp.logical_not(first_owner))
    def _():
        x_copy(held, r, c).wait_recv()

    @pl.when(solver)
    def _():
        y_acc[...] -= dot_nt(held[...], factor[lead + kd])

        @pl.when(c + 1 <= last)
        def _():
            src = jnp.minimum(c + 1, last)
            part_copy(0, src, c).wait_recv()
            y_acc[...] -= parts[src].astype(F32)

        solved[kd] = times_inverse(y_acc[...], inv[kd]).astype(BF16)
        for dr in range(1, grid_rows + 1):
            row = lax.rem(r - dr + 2 * grid_rows, grid_rows)
            x_copy(solved.at[kd], row, k).start()

    for d in reversed(range(diag)):
        block = d * grid_rows + r

        @pl.when(block < k)
        def _():
            part_out[d] = dot_nt(held[...], factor[lead + d]).astype(BF16)
            part_copy(d, c, block + 1).start()

    loads[3].wait()
    per_block = pieces // lead
    rows = nrhs // per_block

    def lead_step(t, carry):
        product = dot_nt(held[...], factor[t]).astype(BF16)
        for q in range(per_block):
            piece = t * per_block + q
            lead_out[piece] = product[q * rows : (q + 1) * rows]

            @pl.when(piece != c)
            def _():
                lead_copy(piece, c).start()

        return carry

    lax.fori_loop(0, lead, lead_step, 0)

    @pl.when(solver)
    def _():
        def send(step, carry):
            solved_copy(kd, lax.rem(c + step, grid_cols)).start()
            return carry

        lax.fori_loop(1, grid_cols, send, 0)

    def add_lead(step, total):
        src = last - step

        @pl.when(src != c)
        def _():
            lead_copy(c, src).wait_recv()

        @pl.when(src == c)
        def _():
            lead_in[src] = lead_out[c]

        return total + lead_in[src].astype(F32)

    total = lax.fori_loop(0, grid_cols, add_lead, jnp.zeros(lead_in.shape[1:], F32))
    sums[c] = total.astype(BF16)

    def send_sum(step, carry):
        sum_copy(c, lax.rem(c + step, grid_cols)).start()
        return carry

    lax.fori_loop(1, grid_cols, send_sum, 0)

    for d in range(diag):
        block = d * grid_rows + r

        @pl.when(jnp.logical_and(block != last, block + 1 != c))
        def _():
            solved_copy(d, c).wait_recv()

        out[lead + d] = solved[d]

    def wait_sum(step, carry):
        sum_copy(lax.rem(c + step, grid_cols), c).wait_recv()
        return carry

    lax.fori_loop(1, grid_cols, wait_sum, 0)
    for t in range(lead):
        for q in range(per_block):
            out[t, q * rows : (q + 1) * rows] = sums[t * per_block + q]

    @pl.when(first_owner)
    def _():
        for dr in range(1, grid_rows):
            x_copy(solved.at[last_slot], (last_row + dr) % grid_rows, last).wait_send()

    @pl.when(solver)
    def _():
        for row in range(grid_rows):
            x_copy(solved.at[kd], row, k).wait_send()

        def sent(step, carry):
            solved_copy(kd, lax.rem(c + step, grid_cols)).wait_send()
            return carry

        lax.fori_loop(1, grid_cols, sent, 0)

    for d in range(diag):
        block = d * grid_rows + r

        @pl.when(block < k)
        def _():
            part_copy(d, c, block + 1).wait_send()

    def all_sent(step, carry):
        other = lax.rem(c + step, grid_cols)
        lead_copy(other, c).wait_send()
        sum_copy(c, other).wait_send()
        return carry

    lax.fori_loop(1, grid_cols, all_sent, 0)


def shards(factor, dinv, rhs):
    grid_rows = lax.axis_size("row")
    grid_cols = lax.axis_size("col")
    tiles = factor.reshape(factor.shape[1], factor.shape[2], factor.shape[4])
    inverse = dinv[0]
    local_rhs = rhs[0]
    held_rows, nrhs, order = local_rhs.shape
    diag = inverse.shape[0]
    lead = held_rows - diag
    pieces = grid_cols
    assert pieces % lead == 0 and (lead * nrhs) % (16 * pieces) == 0
    rows = lead * nrhs // pieces
    dma = pltpu.SemaphoreType.DMA
    update = pl.pallas_call(
        functools.partial(kernel, grid_rows, grid_cols, lead, diag, nrhs, pieces),
        out_shape=jax.ShapeDtypeStruct((held_rows, nrhs, order), BF16),
        in_specs=[pl.BlockSpec(memory_space=pl.ANY)] * 3,
        out_specs=pl.BlockSpec(memory_space=pltpu.VMEM),
        scratch_shapes=[
            pltpu.VMEM(tiles.shape, BF16),
            pltpu.VMEM(inverse.shape, BF16),
            pltpu.VMEM(local_rhs.shape, F32),
            pltpu.VMEM((nrhs, order), BF16),
            pltpu.VMEM((grid_cols, nrhs, order), BF16),
            pltpu.VMEM((diag, nrhs, order), BF16),
            pltpu.VMEM((pieces, rows, order), BF16),
            pltpu.VMEM((grid_cols, rows, order), BF16),
            pltpu.VMEM((pieces, rows, order), BF16),
            pltpu.VMEM((diag, nrhs, order), BF16),
            pltpu.VMEM((nrhs, order), F32),
            dma((4,)),
            dma((grid_rows,)),
            dma,
            dma((diag,)),
            dma((grid_cols,)),
            dma((pieces,)),
            dma((grid_cols,)),
            dma((grid_cols,)),
            dma((grid_cols,)),
            dma((grid_cols,)),
            dma((diag,)),
        ],
        compiler_params=pltpu.CompilerParams(
            collective_id=0, has_side_effects=True, vmem_limit_bytes=48 * 1024 * 1024
        ),
        cost_estimate=pl.CostEstimate(
            flops=2 * held_rows * nrhs * order * order,
            bytes_accessed=2 * held_rows * order * order,
            transcendentals=0,
        ),
    )(tiles, inverse, local_rhs).astype(F32)
    leading = lax.broadcasted_iota(jnp.int32, (held_rows, 1, 1), 0) < lead
    return jnp.where(leading, local_rhs - update, update)[None]


def solution(mesh):
    in_specs = (
        P("row", None, None, "col", None),
        P("row", None, None, None),
        P("row", None, None, None),
    )
    out_specs = P("row", None, None, None)
    return jax.shard_map(shards, mesh=mesh, in_specs=in_specs, out_specs=out_specs, check_vma=False)
```

time: 981 us -> 66.3 us (0.07)
  waiting for transfers between devices: 905 us -> 0 us
  Pallas kernels: 0 us -> 62.1 us
  matrix products: 22.9 us -> 0 us
  other arithmetic: 18.6 us -> 1.42 us
  local copies, waits for them, and re-layouts: 17.3 us -> 2.54 us
  between operations: 14.5 us -> 0.01 us
    psum x17 -> x0, waiting for transfers between devices: 905 us -> none  [the longest x8 586 us: one_step(): summed = lax.psum(partials[tile_slot], 'col')]
    pallas_call x0 -> x1, Pallas kernels: none -> 62.1 us  [shards(): pl.pallas_call(functools.partial(kernel, grid_rows, grid_cols, lead, diag...]
    dot_general x9 -> x0, matrix products: 22.9 us -> none  [the longest x8 18.7 us: one_step(): jnp.dot(y_block, tile_inv.astype(jnp.float32).T, precision=lax.Precision....]
    scatter x9 -> x0, other arithmetic: 12.8 us -> none  [the longest x8 10.4 us: one_step(): results.at[tile_slot]]
  transfers between devices with their start and end apart: 17 -> 0, of which waited for: 17 -> 0; matrix products, arithmetic and copies ran while one was open for 2% -> 0% of each run, Pallas kernels for 0% -> 0%
where the time goes in v1:
time: 66.3 us; the launch traced here: 66.1 us
  Pallas kernels  62.1 us (94%)
  local copies, waits for them, and re-layouts  2.54 us (4%)
  other arithmetic  1.42 us (2%)
    pallas_call x1, Pallas kernels, shards(): pl.pallas_call(functools.partial(kernel, grid_rows, grid_cols, lead, diag...  62.1 us
    unnamed x4, local copies, waits for them, and re-layouts  2.54 us
    broadcast_in_dim x1, other arithmetic, shards(): return jnp.where(leading, local_rhs - update, update)[None]  1.42 us

profile of v1, /device:TPU:8, one launch (start us, length us, event | category | flops | bytes accessed | tf_op | source)
XLA Modules:
  0.0 66.1 jit_solution(1184879968197328312)
XLA Ops:
  0.0 0.0 copy-start
  0.0 1.3 %copy-done = f32[1,10,64,512]{3,2,1,0:T(8,128)S(1)} copy-done((f32[1,10,64,512]{3,2,1,0:T(8,128)S(1)}, f32[1,10,64,512]{3,2,1,0:T(8,128)}, u32[]{:S(2)}) %copy-start) | copy-done | bytes 1310744
  1.3 0.0 copy-start.1
  1.3 1.2 %copy-done.1 = bf16[1,2,512,512]{3,2,1,0:T(8,128)(2,1)S(1)} copy-done((bf16[1,2,512,512]{3,2,1,0:T(8,128)(2,1)S(1)}, bf16[1,2,512,512]{3,2,1,0:T(8,128)(2,1)}, u32[]{:S(2)}) %copy-start.1) | copy-done | bytes 1048600
  2.5 62.1 %shard_map.37 = bf16[10,64,512]{2,1,0:T(8,128)(2,1)S(1)} custom-call(bf16[10,512,512]{2,1,0:T(8,128)(2,1)} %bitcast.8, bf16[2,512,512]{2,1,0:T(8,128)(2,1)S(1)} %bitcast.7, f32[10,64,512]{2,1,0:T(8,128)S(1)} %bitcast.6), custom_call_target="tpu_custom_call" | custom-call | flops 335544320 | bytes 5242880 | tf_op jit(solution)/shard_map/pallas_call | solution.py:265
  64.7 1.4 %fusion = f32[1,10,64,512]{3,2,1,0:T(8,128)} fusion(bf16[10,64,512]{2,1,0:T(8,128)(2,1)S(1)} %shard_map.37, pred[10]{0:T(512)(128)(4,1)S(1)} %iota_compare_fusion, f32[1,10,64,512]{3,2,1,0:T(8,128)S(1)} %copy-done), kind=kLoop, calls=%fused_computation.1 | loop fusion | flops 983040 | bytes 3276810 | tf_op jit(solution)/shard_map/broadcast_in_dim | solution.py:304
  (1 shorter events, 0.0 us)
Async XLA Ops:
  0.0 1.3 %copy-start = (f32[1,10,64,512]{3,2,1,0:T(8,128)S(1)}, f32[1,10,64,512]{3,2,1,0:T(8,128)}, u32[]{:S(2)}) copy-start(f32[1,10,64,512]{3,2,1,0:T(8,128)} %param.5) | copy-start | bytes 3932164
  1.3 1.2 %copy-start.1 = (bf16[1,2,512,512]{3,2,1,0:T(8,128)(2,1)S(1)}, bf16[1,2,512,512]{3,2,1,0:T(8,128)(2,1)}, u32[]{:S(2)}) copy-start(bf16[1,2,512,512]{3,2,1,0:T(8,128)(2,1)} %param.4) | copy-start | bytes 3145732

commit v2 on v1

--- a/solution.py
+++ b/solution.py
@@ -28,7 +28,7 @@
     grid_rows, grid_cols, lead, diag, nrhs, pieces,
     factor_in, inv_in, rhs_in, out,
     factor, inv, rhs, held, parts, part_out, lead_out, lead_in, sums, solved, y_acc,
-    load_sem, x_send, x_recv, p_send, p_recv, l_send, l_recv, s_send, s_recv, r_send, r_recv,
+    held_two, tile_two, pair_in, q_recv, h_recv, t_send, t_recv, load_sem, x_send, x_recv, p_send, p_recv, l_send, l_recv, s_send, s_recv, r_send, r_recv, relay_send,
 ):
     r = lax.axis_index("row")
     c = lax.axis_index("col")
@@ -53,20 +53,57 @@
             barrier, inc=1, device_id=(r, lax.rem(c + step, grid_cols)), device_id_type=MESH
         )
     for dr in range(1, grid_rows):
-        for dc in (grid_cols - 1, 0, 1):
+        for dc in (grid_cols - 2, grid_cols - 1, 0, 1, 2):
             pl.semaphore_signal(
                 barrier,
                 inc=1,
                 device_id=(lax.rem(r + dr, grid_rows), lax.rem(c + dc, grid_cols)),
                 device_id_type=MESH,
             )
-    pl.semaphore_wait(barrier, grid_cols - 1 + 3 * (grid_rows - 1))
-
-    def x_copy(src, row, col):
-        return pltpu.make_async_remote_copy(
-            src_ref=src, dst_ref=held, send_sem=x_send.at[row], recv_sem=x_recv,
+    pl.semaphore_wait(barrier, grid_cols - 1 + 5 * (grid_rows - 1))
+
+    chips = grid_rows // 2
+
+    two_row = jnp.logical_and(c >= 2, r == lax.rem(c - 2 + grid_rows, grid_rows))
+
+    def two_copy():
+        block = lax.div(jnp.maximum(c - 2, 0), grid_rows)
+        return pltpu.make_async_remote_copy(
+            src_ref=factor_in.at[lead + block], dst_ref=tile_two, send_sem=t_send,
+            recv_sem=t_recv, device_id=(r, jnp.maximum(c - 1, 0)), device_id_type=MESH,
+        )
+
+    @pl.when(two_row)
+    def _():
+        two_copy().start()
+
+    def x_copy(src, row, col, sem):
+        return pltpu.make_async_remote_copy(
+            src_ref=src, dst_ref=held, send_sem=x_send.at[sem], recv_sem=x_recv,
             device_id=(row, col), device_id_type=MESH,
         )
+
+    def two_x_copy(src, row, col):
+        return pltpu.make_async_remote_copy(
+            src_ref=src, dst_ref=held_two, send_sem=x_send.at[chips], recv_sem=h_recv,
+            device_id=(row, col), device_id_type=MESH,
+        )
+
+    def x_copies(src, column, row, act):
+        after = lax.rem(row + grid_rows - 1, grid_rows)
+        act(x_copy(src, after, column, 0))
+
+        @pl.when(column >= 2)
+        def _():
+            act(
+                two_x_copy(
+                    src, lax.rem(row + grid_rows - 2, grid_rows), jnp.maximum(column - 1, 0)
+                )
+            )
+
+        for step in range(1, chips):
+            chip = lax.rem(lax.div(after, 2) + step, chips)
+            act(x_copy(src, 2 * chip + 1, column, step))
 
     def part_copy(d, src_col, dst_col):
         return pltpu.make_async_remote_copy(
@@ -86,9 +123,10 @@
             recv_sem=s_recv.at[src_col], device_id=(r, dst_col), device_id_type=MESH,
         )
 
-    def solved_copy(d, dst_col):
-        return pltpu.make_async_remote_copy(
-            src_ref=solved.at[d], dst_ref=solved.at[d], send_sem=r_send.at[dst_col],
+    def solved_copy(d, dst_col, relayed=False):
+        return pltpu.make_async_remote_copy(
+            src_ref=solved.at[d], dst_ref=solved.at[d],
+            send_sem=relay_send.at[d] if relayed else r_send.at[dst_col],
             recv_sem=r_recv.at[d], device_id=(r, dst_col), device_id_type=MESH,
         )
 
@@ -102,8 +140,7 @@
 
     @pl.when(first_owner)
     def _():
-        for dr in range(1, grid_rows):
-            x_copy(solved.at[last_slot], (last_row + dr) % grid_rows, last).start()
+        x_copies(solved.at[last_slot], last, last_row, lambda copy: copy.start())
         held[...] = solved[last_slot]
 
     loads[2].wait()
@@ -119,41 +156,62 @@
         def add(step, carry):
             src = last - step
             part_copy(0, src, c).wait_recv()
-            y_acc[...] -= parts[src].astype(F32)
+            y_acc[...] -= parts[src]
             return carry
 
         lax.fori_loop(0, jnp.maximum(last - c - 1, 0), add, 0)
 
+        @pl.when(c + 1 <= last)
+        def _():
+            two_copy().wait_recv()
+            two_x_copy(held_two, r, c).wait_recv()
+            y_acc[...] -= dot_nt(held_two[...], tile_two[...])
+
     @pl.when(jnp.logical_not(first_owner))
     def _():
-        x_copy(held, r, c).wait_recv()
+        x_copy(held, r, c, 0).wait_recv()
+
+    after = lax.rem(c - 1 + grid_rows, grid_rows)
+    lead_of_chip = jnp.where(
+        lax.div(r, 2) == lax.div(after, 2), r == after, lax.rem(r, 2) == 1
+    )
+    relay = jnp.logical_and(
+        lead_of_chip, jnp.logical_not(jnp.logical_and(c == last, lax.div(r, 2) == last_row // 2))
+    )
+    sibling = r + 1 - 2 * lax.rem(r, 2)
+
+    @pl.when(relay)
+    def _():
+        x_copy(held, sibling, c, chips + 1).start()
 
     @pl.when(solver)
     def _():
         y_acc[...] -= dot_nt(held[...], factor[lead + kd])
-
-        @pl.when(c + 1 <= last)
-        def _():
-            src = jnp.minimum(c + 1, last)
-            part_copy(0, src, c).wait_recv()
-            y_acc[...] -= parts[src].astype(F32)
-
         solved[kd] = times_inverse(y_acc[...], inv[kd]).astype(BF16)
-        for dr in range(1, grid_rows + 1):
-            row = lax.rem(r - dr + 2 * grid_rows, grid_rows)
-            x_copy(solved.at[kd], row, k).start()
+        x_copies(solved.at[kd], k, r, lambda copy: copy.start())
 
     for d in reversed(range(diag)):
         block = d * grid_rows + r
 
-        @pl.when(block < k)
-        def _():
-            part_out[d] = dot_nt(held[...], factor[lead + d]).astype(BF16)
+        @pl.when(block < k - 1)
+        def _():
+            part_out[d] = dot_nt(held[...], factor[lead + d])
             part_copy(d, c, block + 1).start()
 
     loads[3].wait()
     per_block = pieces // lead
+    pair = c + 1 - 2 * lax.rem(c, 2)
+    parity = lax.rem(c, 2)
+    half = grid_cols // 2
     rows = nrhs // per_block
+    early = c >= 2
+
+    def pair_copy(piece):
+        return pltpu.make_async_remote_copy(
+            src_ref=lead_out.at[piece], dst_ref=pair_in.at[lax.div(piece, 2)],
+            send_sem=l_send.at[piece], recv_sem=q_recv.at[lax.div(piece, 2)],
+            device_id=(r, pair), device_id_type=MESH,
+        )
 
     def lead_step(t, carry):
         product = dot_nt(held[...], factor[t]).astype(BF16)
@@ -161,24 +219,46 @@
             piece = t * per_block + q
             lead_out[piece] = product[q * rows : (q + 1) * rows]
 
+            @pl.when(jnp.logical_and(early, lax.rem(piece, 2) != parity))
+            def _():
+                pair_copy(piece).start()
+
+            @pl.when(jnp.logical_and(jnp.logical_not(early), piece != c))
+            def _():
+                lead_copy(piece, c).start()
+
+        return carry
+
+    lax.fori_loop(0, lead, lead_step, 0)
+
+    @pl.when(solver)
+    def _():
+        def send(step, carry):
+            solved_copy(kd, lax.rem(c + 2 * step, grid_cols)).start()
+            return carry
+
+        solved_copy(kd, pair).start()
+        lax.fori_loop(1, half, send, 0)
+
+    @pl.when(early)
+    def _():
+        def join(m, carry):
+            piece = 2 * m + parity
+            pair_copy(piece).wait_recv()
+            lead_out[piece] = (
+                lead_out[piece].astype(F32) + pair_in[m].astype(F32)
+            ).astype(BF16)
+
             @pl.when(piece != c)
             def _():
                 lead_copy(piece, c).start()
 
-        return carry
-
-    lax.fori_loop(0, lead, lead_step, 0)
-
-    @pl.when(solver)
-    def _():
-        def send(step, carry):
-            solved_copy(kd, lax.rem(c + step, grid_cols)).start()
             return carry
 
-        lax.fori_loop(1, grid_cols, send, 0)
+        lax.fori_loop(0, half, join, 0)
 
     def add_lead(step, total):
-        src = last - step
+        src = jnp.where(step < half - 1, 2 * (half - 1 - step) + parity, half - step)
 
         @pl.when(src != c)
         def _():
@@ -190,7 +270,7 @@
 
         return total + lead_in[src].astype(F32)
 
-    total = lax.fori_loop(0, grid_cols, add_lead, jnp.zeros(lead_in.shape[1:], F32))
+    total = lax.fori_loop(0, half + 1, add_lead, jnp.zeros(lead_in.shape[1:], F32))
     sums[c] = total.astype(BF16)
 
     def send_sum(step, carry):
@@ -205,6 +285,10 @@
         @pl.when(jnp.logical_and(block != last, block + 1 != c))
         def _():
             solved_copy(d, c).wait_recv()
+
+            @pl.when(lax.rem(block + 1, 2) == parity)
+            def _():
+                solved_copy(d, pair, True).start()
 
         out[lead + d] = solved[d]
 
@@ -217,26 +301,41 @@
         for q in range(per_block):
             out[t, q * rows : (q + 1) * rows] = sums[t * per_block + q]
 
+    @pl.when(two_row)
+    def _():
+        two_copy().wait_send()
+
+    @pl.when(relay)
+    def _():
+        x_copy(held, sibling, c, chips + 1).wait_send()
+
     @pl.when(first_owner)
     def _():
-        for dr in range(1, grid_rows):
-            x_copy(solved.at[last_slot], (last_row + dr) % grid_rows, last).wait_send()
+        x_copies(solved.at[last_slot], last, last_row, lambda copy: copy.wait_send())
 
     @pl.when(solver)
     def _():
-        for row in range(grid_rows):
-            x_copy(solved.at[kd], row, k).wait_send()
+        x_copies(solved.at[kd], k, r, lambda copy: copy.wait_send())
 
         def sent(step, carry):
-            solved_copy(kd, lax.rem(c + step, grid_cols)).wait_send()
+            solved_copy(kd, lax.rem(c + 2 * step, grid_cols)).wait_send()
             return carry
 
-        lax.fori_loop(1, grid_cols, sent, 0)
+        solved_copy(kd, pair).wait_send()
+        lax.fori_loop(1, half, sent, 0)
 
     for d in range(diag):
         block = d * grid_rows + r
-
-        @pl.when(block < k)
+        other = jnp.logical_and(block != last, block + 1 != c)
+
+        @pl.when(jnp.logical_and(other, lax.rem(block + 1, 2) == parity))
+        def _():
+            solved_copy(d, pair, True).wait_send()
+
+    for d in range(diag):
+        block = d * grid_rows + r
+
+        @pl.when(block < k - 1)
         def _():
             part_copy(d, c, block + 1).wait_send()
 
@@ -259,6 +358,8 @@
     diag = inverse.shape[0]
     lead = held_rows - diag
     pieces = grid_cols
+    assert grid_rows % 2 == 0 and grid_cols % grid_rows == 0 and grid_cols >= 5
+    assert grid_cols % 2 == 0
     assert pieces % lead == 0 and (lead * nrhs) % (16 * pieces) == 0
     rows = lead * nrhs // pieces
     dma = pltpu.SemaphoreType.DMA
@@ -272,15 +373,22 @@
             pltpu.VMEM(inverse.shape, BF16),
             pltpu.VMEM(local_rhs.shape, F32),
             pltpu.VMEM((nrhs, order), BF16),
-            pltpu.VMEM((grid_cols, nrhs, order), BF16),
-            pltpu.VMEM((diag, nrhs, order), BF16),
+            pltpu.VMEM((grid_cols, nrhs, order), F32),
+            pltpu.VMEM((diag, nrhs, order), F32),
             pltpu.VMEM((pieces, rows, order), BF16),
             pltpu.VMEM((grid_cols, rows, order), BF16),
             pltpu.VMEM((pieces, rows, order), BF16),
             pltpu.VMEM((diag, nrhs, order), BF16),
             pltpu.VMEM((nrhs, order), F32),
+            pltpu.VMEM((nrhs, order), BF16),
+            pltpu.VMEM((order, order), BF16),
+            pltpu.VMEM((grid_cols // 2, rows, order), BF16),
+            dma((grid_cols // 2,)),
+            dma,
+            dma,
+            dma,
             dma((4,)),
-            dma((grid_rows,)),
+            dma((grid_rows // 2 + 2,)),
             dma,
             dma((diag,)),
             dma((grid_cols,)),
@@ -290,9 +398,10 @@
             dma((grid_cols,)),
             dma((grid_cols,)),
             dma((diag,)),
+            dma((diag,)),
         ],
         compiler_params=pltpu.CompilerParams(
-            collective_id=0, has_side_effects=True, vmem_limit_bytes=48 * 1024 * 1024
+            collective_id=0, has_side_effects=True, vmem_limit_bytes=60 * 1024 * 1024
         ),
         cost_estimate=pl.CostEstimate(
             flops=2 * held_rows * nrhs * order * order,

time: 66.3 us -> 61.8 us (0.932)
  Pallas kernels: 62.1 us -> 59.1 us
  local copies, waits for them, and re-layouts: 2.54 us -> 0.01 us
  other arithmetic: 1.42 us -> 2.52 us
    pallas_call x1, Pallas kernels: 62.1 us -> 59.1 us  [shards(): pl.pallas_call(functools.partial(kernel, grid_rows, grid_cols, lead, diag...]
    unnamed x4 -> x2, local copies, waits for them, and re-layouts: 2.54 us -> 0.01 us
    broadcast_in_dim x1, other arithmetic: 1.42 us -> 2.52 us  [shards(): return jnp.where(leading, local_rhs - update, update)[None]]
where the time goes in v2:
time: 61.8 us; the launch traced here: 61.7 us
  Pallas kernels  59.1 us (96%)
  other arithmetic  2.52 us (4%)
    pallas_call x1, Pallas kernels, shards(): pl.pallas_call(functools.partial(kernel, grid_rows, grid_cols, lead, diag...  59.1 us
    broadcast_in_dim x1, other arithmetic, shards(): return jnp.where(leading, local_rhs - update, update)[None]  2.52 us

profile of v2, /device:TPU:8, one launch (start us, length us, event | category | flops | bytes accessed | tf_op | source)
XLA Modules:
  0.0 61.7 jit_solution(7884772585267412804)
XLA Ops:
  0.0 0.0 copy-start
  0.0 59.1 %shard_map.37 = bf16[10,64,512]{2,1,0:T(8,128)(2,1)} custom-call(bf16[10,512,512]{2,1,0:T(8,128)(2,1)} %bitcast.7, bf16[2,512,512]{2,1,0:T(8,128)(2,1)} %bitcast.8, f32[10,64,512]{2,1,0:T(8,128)} %bitcast.6), custom_call_target="tpu_custom_call" | custom-call | flops 335544320 | bytes 5242880 | tf_op jit(solution)/shard_map/pallas_call | solution.py:366
  59.1 0.0 copy-done
  59.2 2.5 %fusion = f32[1,10,64,512]{3,2,1,0:T(8,128)} fusion(bf16[10,64,512]{2,1,0:T(8,128)(2,1)} %shard_map.37, pred[10]{0:T(512)(128)(4,1)S(1)} %iota_compare_fusion, f32[1,10,64,512]{3,2,1,0:T(8,128)S(1)} %copy-done), kind=kLoop, calls=%fused_computation.1 | loop fusion | flops 983040 | bytes 3276810 | tf_op jit(solution)/shard_map/broadcast_in_dim | solution.py:413
  (1 shorter events, 0.0 us)
Async XLA Ops:
  0.0 59.1 %copy-start = (f32[1,10,64,512]{3,2,1,0:T(8,128)S(1)}, f32[1,10,64,512]{3,2,1,0:T(8,128)}, u32[]{:S(2)}) copy-start(f32[1,10,64,512]{3,2,1,0:T(8,128)} %param.5) | copy-start | bytes 3932164
